TPU v7x, 512 devices: a whole 4x4x16 slice. The times are simulated.
512 devices in a mesh: section: 8 (over y, core), chan: 16 (over z), rep: 4 (over x).
Axes of the slice: x: 4, y: 4, z: 16, core: 2. Of those that a mesh axis runs over, the one named last changes fastest.
Arguments:
- latent: bfloat16 [8, 1280, 64], P('rep', 'chan'), parts along dimension 0, may hold values from -6 to 6
- stale_rows: bfloat16 [4, 8, 8, 1280, 2, 32], P(None, 'section', 'rep', 'chan'), parts along dimension 2, may hold values from -5 to 5
- conv_weight: bfloat16 [8, 9, 1280, 1280], P('section', None, 'chan'), may hold values from -0.078125 to 0.078125
- conv_bias: float32 [8, 1280], P('section', 'chan'), may hold values from -1.5 to 1.5
- norm_gain: float32 [8, 1280], P('section', 'chan'), may hold values from 0.5 to 1.5
- norm_shift: float32 [8, 1280], P('section', 'chan'), may hold values from -2.5 to 2.5
- time_proj: bfloat16 [8, 320, 1280], P('section', None, 'chan'), may hold values from -0.3125 to 0.3125
- patch_order: int32 [2], replicated, may hold values from 0 to 1, each once
- timestep: int32 [4], P('rep'), parts along dimension 0, may hold values from 0 to 999
- stale_step: int32 [8, 2], P('section'), may hold values from 0 to 3
Outputs:
- segment_out: bfloat16 [8, 8, 1280, 64], P('section', 'rep', 'chan'), parts along dimension 1
There are 4 independent parts, one for each index of `rep`. A program takes and returns all parts, laid end to end along the dimension named above; an argument that names none is the same for every part. Nothing has to cross between parts.
Inputs may be any that keep to these rules, and one draw needn't show every extreme that they name: `patch_order`: each patch appears once.
All inputs are finite; a program needn't handle non-finite values.
Results may differ from a plain program's by a relative error of at most 0.017.
Values may be sent and summed in bfloat16 or wider, within the bound.
A program may use at most 64 MiB of HBM per device.

v0:
```python
import math

import jax
import jax.numpy as jnp
from jax import lax
from jax.sharding import PartitionSpec as P

C = 1280
GROUPS = 32
TDIM = 320
HP = 2
W = 32


def passed_along(block, axis, distance):
    devices = range(lax.axis_size(axis))
    route = [(i - distance, i) for i in devices if i - distance in devices]
    return lax.ppermute(block, axis, route)


def tap_stack(extended, rows, cols):
    taps = jnp.stack(
        [extended[:, a : a + rows, b : b + cols] for a in range(3) for b in range(3)], axis=0
    )
    return taps.reshape(9, extended.shape[0], rows * cols)


def pick_bank(stale_rows, stale_step):
    levels = jnp.arange(stale_rows.shape[0], dtype=jnp.int32)
    chosen = (stale_step[None, :, :] == levels[:, None, None])[:, :, :, None, None, None]
    picked = jnp.where(chosen, stale_rows.astype(jnp.float32), jnp.float32(0.0))
    return jnp.sum(picked, axis=0).astype(jnp.bfloat16)


def on_device(
    latent,
    stale_rows,
    conv_weight,
    conv_bias,
    norm_gain,
    norm_shift,
    time_proj,
    patch_order,
    timestep,
    stale_step,
):
    patches = latent.shape[0]
    local_chan = latent.shape[1]
    cells = HP * W
    group_size = C // GROUPS
    section = lax.axis_index("section")
    sections = lax.axis_size("section")
    index = jnp.arange(patches, dtype=jnp.int32)
    rank = jnp.sum(jnp.where(patch_order[:, None] == index[None, :], index[:, None], 0), axis=0)
    half = TDIM // 2
    freqs = jnp.exp(-math.log(10000.0) * jnp.arange(half, dtype=jnp.float32) / half)
    angles = timestep.astype(jnp.float32)[0] * freqs
    emb = jnp.concatenate([jnp.cos(angles), jnp.sin(angles)])
    semb = jax.nn.silu(emb).astype(jnp.bfloat16)[None, :]
    temb = jnp.dot(semb, time_proj[0], preferred_element_type=jnp.float32)[0]
    bank = pick_bank(stale_rows, stale_step)[0]
    gain = norm_gain[0][:, None]
    shift_term = norm_shift[0][:, None]
    extra = conv_bias[0][:, None] + temb[:, None]
    local_weight = conv_weight[0]

    def slot_step(slot, carry):
        incoming, hidden_buf, out_buf = carry
        position = slot - section
        valid = (position >= 0) & (position < patches)
        place = jnp.clip(position, 0, patches - 1)
        patch = lax.dynamic_index_in_dim(patch_order, place, 0, keepdims=False)
        first = lax.dynamic_index_in_dim(latent, patch, 0, keepdims=False)
        x_in = jnp.where(section == 0, first, incoming)
        xf = x_in.astype(jnp.float32)
        grouped = xf.reshape(local_chan // group_size, group_size * cells)
        mean = jnp.mean(grouped, axis=1, keepdims=True)
        var = jnp.mean((grouped - mean) ** 2, axis=1, keepdims=True)
        normed = ((grouped - mean) / jnp.sqrt(var + 1e-05)).reshape(local_chan, cells)
        hidden = (
            jax.nn.silu(normed * gain + shift_term).astype(jnp.bfloat16).reshape(local_chan, HP, W)
        )
        older = lax.dynamic_index_in_dim(hidden_buf, patch, 0, keepdims=False)
        hidden_buf = lax.dynamic_update_index_in_dim(
            hidden_buf, jnp.where(valid, hidden, older), patch, 0
        )
        above = jnp.maximum(patch - 1, 0)
        below = jnp.minimum(patch + 1, patches - 1)
        rank_above = lax.dynamic_index_in_dim(rank, above, 0, keepdims=False)
        rank_below = lax.dynamic_index_in_dim(rank, below, 0, keepdims=False)
        top_new = lax.dynamic_index_in_dim(hidden_buf, above, 0, keepdims=False)[:, HP - 1, :]
        top_old = lax.dynamic_index_in_dim(bank, above, 0, keepdims=False)[:, 1, :]
        top = jnp.where(rank_above < place, top_new, top_old)
        top = jnp.where(patch > 0, top, jnp.zeros_like(top))
        bottom_new = lax.dynamic_index_in_dim(hidden_buf, below, 0, keepdims=False)[:, 0, :]
        bottom_old = lax.dynamic_index_in_dim(bank, below, 0, keepdims=False)[:, 0, :]
        bottom = jnp.where(rank_below < place, bottom_new, bottom_old)
        bottom = jnp.where(patch < patches - 1, bottom, jnp.zeros_like(bottom))
        extended = jnp.concatenate([top[:, None, :], hidden, bottom[:, None, :]], axis=1)
        extended = jnp.pad(extended, ((0, 0), (0, 0), (1, 1)))
        taps = tap_stack(extended, HP, W).reshape(9 * local_chan, cells)
        partial_out = lax.dot_general(
            local_weight.reshape(9 * local_chan, C),
            taps,
            (((0,), (0,)), ((), ())),
            preferred_element_type=jnp.float32,
        )
        conv = lax.psum_scatter(partial_out, "chan", scatter_dimension=0, tiled=True)
        result = (xf + conv + extra).astype(jnp.bfloat16)
        kept = lax.dynamic_index_in_dim(out_buf, patch, 0, keepdims=False)
        out_buf = lax.dynamic_update_index_in_dim(out_buf, jnp.where(valid, result, kept), patch, 0)
        passed = passed_along(result, "section", 1)
        return (passed, hidden_buf, out_buf)

    start_state = (
        jnp.zeros((local_chan, cells), jnp.bfloat16),
        jnp.zeros((patches, local_chan, HP, W), jnp.bfloat16),
        jnp.zeros((patches, local_chan, cells), jnp.bfloat16),
    )
    final_state = lax.fori_loop(0, patches + sections - 1, slot_step, start_state)
    return final_state[2][None]


def solution(mesh):
    placed = (
        P("rep", "chan", None),
        P(None, "section", "rep", "chan", None, None),
        P("section", None, "chan", None),
        P("section", "chan"),
        P("section", "chan"),
        P("section", "chan"),
        P("section", None, "chan"),
        P(),
        P("rep"),
        P("section", None),
    )
    return jax.shard_map(
        on_device,
        mesh=mesh,
        in_specs=placed,
        out_specs=P("section", "rep", "chan", None),
        check_vma=False,
    )
```

profile of v0, /device:TPU:25, one launch (start us, length us, event | category | flops | bytes accessed | tf_op | source)
XLA Modules:
  0.0 808.1 jit_solution(14417958475974058861)
XLA Ops:
  10.6 790.3 %while.19 = (s32[]{:T(128)}, bf16[80,64]{0,1:T(8,128)(2,1)S(1)}, bf16[2,80,2,32]{1,3,2,0:T(8,128)(2,1)S(1)}, bf16[2,80,64]{1,2,0:T(8,128)(2,1)S(1)}, pred[]{:T(5...) while((s32[]{:T(128)}, bf16[80,64]{0,1:T(8,128)(2,1)S(1)}, ...), condition=%wide.region_8.9_spmd, body=%wide.region_2.8_spmd.sunk | while | flops 118264344 | bytes 5458201 | solution.py:120
  10.7 1.3 dynamic_slice.124
  21.6 1.9 convolution_bitcast_fusion.3
  24.7 63.3 %reduce-scatter.6.cloned.1.call-done = f32[80,64]{1,0:T(8,128)} async-done(((f32[1280,64]{1,0:T(8,128)}), f32[80,64]{1,0:T(8,128)}) %reduce-scatter.6.cloned.1.call-update) | async-done | bytes 20496 | tf_op jit(solution)/shard_map/while
  90.2 12.4 %collective-permute-done = bf16[80,64]{0,1:T(8,128)(2,1)S(1)} collective-permute-done((bf16[80,64]{0,1:T(8,128)(2,1)S(1)}, bf16[80,64]{0,1:T(8,128)(2,1)S(1)}, u32[]{:S(2)}, u32[]{:S(2)}) %collective-permute-start) | collective-permute-done | bytes 10272 | tf_op jit(solution)/shard_map/while/body/eval_jaxpr/ppermute | solution.py:18
  102.6 1.3 dynamic_slice.124
  113.5 1.9 convolution_bitcast_fusion.3
  116.6 58.8 %reduce-scatter.6.cloned.1.call-done = f32[80,64]{1,0:T(8,128)} async-done(((f32[1280,64]{1,0:T(8,128)}), f32[80,64]{1,0:T(8,128)}) %reduce-scatter.6.cloned.1.call-update) | async-done | bytes 20496 | tf_op jit(solution)/shard_map/while
  177.5 12.5 %collective-permute-done = bf16[80,64]{0,1:T(8,128)(2,1)S(1)} collective-permute-done((bf16[80,64]{0,1:T(8,128)(2,1)S(1)}, bf16[80,64]{0,1:T(8,128)(2,1)S(1)}, u32[]{:S(2)}, u32[]{:S(2)}) %collective-permute-start) | collective-permute-done | bytes 10272 | tf_op jit(solution)/shard_map/while/body/eval_jaxpr/ppermute | solution.py:18
  190.0 1.3 dynamic_slice.124
  200.9 1.9 convolution_bitcast_fusion.3
  204.0 59.1 %reduce-scatter.6.cloned.1.call-done = f32[80,64]{1,0:T(8,128)} async-done(((f32[1280,64]{1,0:T(8,128)}), f32[80,64]{1,0:T(8,128)}) %reduce-scatter.6.cloned.1.call-update) | async-done | bytes 20496 | tf_op jit(solution)/shard_map/while
  265.2 12.1 %collective-permute-done = bf16[80,64]{0,1:T(8,128)(2,1)S(1)} collective-permute-done((bf16[80,64]{0,1:T(8,128)(2,1)S(1)}, bf16[80,64]{0,1:T(8,128)(2,1)S(1)}, u32[]{:S(2)}, u32[]{:S(2)}) %collective-permute-start) | collective-permute-done | bytes 10272 | tf_op jit(solution)/shard_map/while/body/eval_jaxpr/ppermute | solution.py:18
  288.2 1.9 convolution_bitcast_fusion.3
  291.3 59.0 %reduce-scatter.6.cloned.1.call-done = f32[80,64]{1,0:T(8,128)} async-done(((f32[1280,64]{1,0:T(8,128)}), f32[80,64]{1,0:T(8,128)}) %reduce-scatter.6.cloned.1.call-update) | async-done | bytes 20496 | tf_op jit(solution)/shard_map/while
  352.4 12.3 %collective-permute-done = bf16[80,64]{0,1:T(8,128)(2,1)S(1)} collective-permute-done((bf16[80,64]{0,1:T(8,128)(2,1)S(1)}, bf16[80,64]{0,1:T(8,128)(2,1)S(1)}, u32[]{:S(2)}, u32[]{:S(2)}) %collective-permute-start) | collective-permute-done | bytes 10272 | tf_op jit(solution)/shard_map/while/body/eval_jaxpr/ppermute | solution.py:18
  375.6 1.9 convolution_bitcast_fusion.3
  378.7 58.9 %reduce-scatter.6.cloned.1.call-done = f32[80,64]{1,0:T(8,128)} async-done(((f32[1280,64]{1,0:T(8,128)}), f32[80,64]{1,0:T(8,128)}) %reduce-scatter.6.cloned.1.call-update) | async-done | bytes 20496 | tf_op jit(solution)/shard_map/while
  439.8 12.0 %collective-permute-done = bf16[80,64]{0,1:T(8,128)(2,1)S(1)} collective-permute-done((bf16[80,64]{0,1:T(8,128)(2,1)S(1)}, bf16[80,64]{0,1:T(8,128)(2,1)S(1)}, u32[]{:S(2)}, u32[]{:S(2)}) %collective-permute-start) | collective-permute-done | bytes 10272 | tf_op jit(solution)/shard_map/while/body/eval_jaxpr/ppermute | solution.py:18
  462.7 1.9 convolution_bitcast_fusion.3
  465.8 59.1 %reduce-scatter.6.cloned.1.call-done = f32[80,64]{1,0:T(8,128)} async-done(((f32[1280,64]{1,0:T(8,128)}), f32[80,64]{1,0:T(8,128)}) %reduce-scatter.6.cloned.1.call-update) | async-done | bytes 20496 | tf_op jit(solution)/shard_map/while
  527.0 12.1 %collective-permute-done = bf16[80,64]{0,1:T(8,128)(2,1)S(1)} collective-permute-done((bf16[80,64]{0,1:T(8,128)(2,1)S(1)}, bf16[80,64]{0,1:T(8,128)(2,1)S(1)}, u32[]{:S(2)}, u32[]{:S(2)}) %collective-permute-start) | collective-permute-done | bytes 10272 | tf_op jit(solution)/shard_map/while/body/eval_jaxpr/ppermute | solution.py:18
  539.1 1.3 dynamic_slice.124
  550.0 1.9 convolution_bitcast_fusion.3
  553.1 59.0 %reduce-scatter.6.cloned.1.call-done = f32[80,64]{1,0:T(8,128)} async-done(((f32[1280,64]{1,0:T(8,128)}), f32[80,64]{1,0:T(8,128)}) %reduce-scatter.6.cloned.1.call-update) | async-done | bytes 20496 | tf_op jit(solution)/shard_map/while
  614.3 12.0 %collective-permute-done = bf16[80,64]{0,1:T(8,128)(2,1)S(1)} collective-permute-done((bf16[80,64]{0,1:T(8,128)(2,1)S(1)}, bf16[80,64]{0,1:T(8,128)(2,1)S(1)}, u32[]{:S(2)}, u32[]{:S(2)}) %collective-permute-start) | collective-permute-done | bytes 10272 | tf_op jit(solution)/shard_map/while/body/eval_jaxpr/ppermute | solution.py:18
  637.2 1.9 convolution_bitcast_fusion.3
  640.3 58.7 %reduce-scatter.6.cloned.1.call-done = f32[80,64]{1,0:T(8,128)} async-done(((f32[1280,64]{1,0:T(8,128)}), f32[80,64]{1,0:T(8,128)}) %reduce-scatter.6.cloned.1.call-update) | async-done | bytes 20496 | tf_op jit(solution)/shard_map/while
  701.2 12.5 %collective-permute-done = bf16[80,64]{0,1:T(8,128)(2,1)S(1)} collective-permute-done((bf16[80,64]{0,1:T(8,128)(2,1)S(1)}, bf16[80,64]{0,1:T(8,128)(2,1)S(1)}, u32[]{:S(2)}, u32[]{:S(2)}) %collective-permute-start) | collective-permute-done | bytes 10272 | tf_op jit(solution)/shard_map/while/body/eval_jaxpr/ppermute | solution.py:18
  724.7 1.9 convolution_bitcast_fusion.3
  727.7 58.3 %reduce-scatter.6.cloned.1.call-done = f32[80,64]{1,0:T(8,128)} async-done(((f32[1280,64]{1,0:T(8,128)}), f32[80,64]{1,0:T(8,128)}) %reduce-scatter.6.cloned.1.call-update) | async-done | bytes 20496 | tf_op jit(solution)/shard_map/while
  788.2 12.7 %collective-permute-done = bf16[80,64]{0,1:T(8,128)(2,1)S(1)} collective-permute-done((bf16[80,64]{0,1:T(8,128)(2,1)S(1)}, bf16[80,64]{0,1:T(8,128)(2,1)S(1)}, u32[]{:S(2)}, u32[]{:S(2)}) %collective-permute-start) | collective-permute-done | bytes 10272 | tf_op jit(solution)/shard_map/while/body/eval_jaxpr/ppermute | solution.py:18
  (352 shorter events, 70.5 us)
Async XLA Ops:
  6.5 0.8 copy-start
  10.6 77.4 %reduce-scatter.6.cloned.1.call-start = ((), (), s32[]{:S(2)}) async-start(), calls=%async_computation.1 | async-start | bytes 696320 | tf_op jit(solution)/shard_map/while
  88.9 13.7 %collective-permute-start = (bf16[80,64]{0,1:T(8,128)(2,1)S(1)}, bf16[80,64]{0,1:T(8,128)(2,1)S(1)}, u32[]{:S(2)}, u32[]{:S(2)}) collective-permute-start(bf16[80,64]{0,1:T(8,128)(2,1)S(1)} %get-tuple-element.466), channel_id=1, source_target_pairs={{0,64},{64,128},{128,192},{192,256},{256,320},{320,384},{384,448},... | collective-permute-start | bytes 30728 | tf_op jit(solution)/shard_map/while/body/eval_jaxpr/ppermute | solution.py:18
  102.6 72.7 %reduce-scatter.6.cloned.1.call-start = ((), (), s32[]{:S(2)}) async-start(), calls=%async_computation.1 | async-start | bytes 696320 | tf_op jit(solution)/shard_map/while
  176.2 13.8 %collective-permute-start = (bf16[80,64]{0,1:T(8,128)(2,1)S(1)}, bf16[80,64]{0,1:T(8,128)(2,1)S(1)}, u32[]{:S(2)}, u32[]{:S(2)}) collective-permute-start(bf16[80,64]{0,1:T(8,128)(2,1)S(1)} %get-tuple-element.466), channel_id=1, source_target_pairs={{0,64},{64,128},{128,192},{192,256},{256,320},{320,384},{384,448},... | collective-permute-start | bytes 30728 | tf_op jit(solution)/shard_map/while/body/eval_jaxpr/ppermute | solution.py:18
  190.0 73.0 %reduce-scatter.6.cloned.1.call-start = ((), (), s32[]{:S(2)}) async-start(), calls=%async_computation.1 | async-start | bytes 696320 | tf_op jit(solution)/shard_map/while
  263.9 13.4 %collective-permute-start = (bf16[80,64]{0,1:T(8,128)(2,1)S(1)}, bf16[80,64]{0,1:T(8,128)(2,1)S(1)}, u32[]{:S(2)}, u32[]{:S(2)}) collective-permute-start(bf16[80,64]{0,1:T(8,128)(2,1)S(1)} %get-tuple-element.466), channel_id=1, source_target_pairs={{0,64},{64,128},{128,192},{192,256},{256,320},{320,384},{384,448},... | collective-permute-start | bytes 30728 | tf_op jit(solution)/shard_map/while/body/eval_jaxpr/ppermute | solution.py:18
  277.3 73.0 %reduce-scatter.6.cloned.1.call-start = ((), (), s32[]{:S(2)}) async-start(), calls=%async_computation.1 | async-start | bytes 696320 | tf_op jit(solution)/shard_map/while
  351.1 13.6 %collective-permute-start = (bf16[80,64]{0,1:T(8,128)(2,1)S(1)}, bf16[80,64]{0,1:T(8,128)(2,1)S(1)}, u32[]{:S(2)}, u32[]{:S(2)}) collective-permute-start(bf16[80,64]{0,1:T(8,128)(2,1)S(1)} %get-tuple-element.466), channel_id=1, source_target_pairs={{0,64},{64,128},{128,192},{192,256},{256,320},{320,384},{384,448},... | collective-permute-start | bytes 30728 | tf_op jit(solution)/shard_map/while/body/eval_jaxpr/ppermute | solution.py:18
  364.7 72.9 %reduce-scatter.6.cloned.1.call-start = ((), (), s32[]{:S(2)}) async-start(), calls=%async_computation.1 | async-start | bytes 696320 | tf_op jit(solution)/shard_map/while
  438.5 13.3 %collective-permute-start = (bf16[80,64]{0,1:T(8,128)(2,1)S(1)}, bf16[80,64]{0,1:T(8,128)(2,1)S(1)}, u32[]{:S(2)}, u32[]{:S(2)}) collective-permute-start(bf16[80,64]{0,1:T(8,128)(2,1)S(1)} %get-tuple-element.466), channel_id=1, source_target_pairs={{0,64},{64,128},{128,192},{192,256},{256,320},{320,384},{384,448},... | collective-permute-start | bytes 30728 | tf_op jit(solution)/shard_map/while/body/eval_jaxpr/ppermute | solution.py:18
  451.8 73.0 %reduce-scatter.6.cloned.1.call-start = ((), (), s32[]{:S(2)}) async-start(), calls=%async_computation.1 | async-start | bytes 696320 | tf_op jit(solution)/shard_map/while
  525.7 13.4 %collective-permute-start = (bf16[80,64]{0,1:T(8,128)(2,1)S(1)}, bf16[80,64]{0,1:T(8,128)(2,1)S(1)}, u32[]{:S(2)}, u32[]{:S(2)}) collective-permute-start(bf16[80,64]{0,1:T(8,128)(2,1)S(1)} %get-tuple-element.466), channel_id=1, source_target_pairs={{0,64},{64,128},{128,192},{192,256},{256,320},{320,384},{384,448},... | collective-permute-start | bytes 30728 | tf_op jit(solution)/shard_map/while/body/eval_jaxpr/ppermute | solution.py:18
  539.1 73.0 %reduce-scatter.6.cloned.1.call-start = ((), (), s32[]{:S(2)}) async-start(), calls=%async_computation.1 | async-start | bytes 696320 | tf_op jit(solution)/shard_map/while
  613.0 13.4 %collective-permute-start = (bf16[80,64]{0,1:T(8,128)(2,1)S(1)}, bf16[80,64]{0,1:T(8,128)(2,1)S(1)}, u32[]{:S(2)}, u32[]{:S(2)}) collective-permute-start(bf16[80,64]{0,1:T(8,128)(2,1)S(1)} %get-tuple-element.466), channel_id=1, source_target_pairs={{0,64},{64,128},{128,192},{192,256},{256,320},{320,384},{384,448},... | collective-permute-start | bytes 30728 | tf_op jit(solution)/shard_map/while/body/eval_jaxpr/ppermute | solution.py:18
  626.3 72.7 %reduce-scatter.6.cloned.1.call-start = ((), (), s32[]{:S(2)}) async-start(), calls=%async_computation.1 | async-start | bytes 696320 | tf_op jit(solution)/shard_map/while
  699.9 13.8 %collective-permute-start = (bf16[80,64]{0,1:T(8,128)(2,1)S(1)}, bf16[80,64]{0,1:T(8,128)(2,1)S(1)}, u32[]{:S(2)}, u32[]{:S(2)}) collective-permute-start(bf16[80,64]{0,1:T(8,128)(2,1)S(1)} %get-tuple-element.466), channel_id=1, source_target_pairs={{0,64},{64,128},{128,192},{192,256},{256,320},{320,384},{384,448},... | collective-permute-start | bytes 30728 | tf_op jit(solution)/shard_map/while/body/eval_jaxpr/ppermute | solution.py:18
  713.8 72.3 %reduce-scatter.6.cloned.1.call-start = ((), (), s32[]{:S(2)}) async-start(), calls=%async_computation.1 | async-start | bytes 696320 | tf_op jit(solution)/shard_map/while
  786.9 14.0 %collective-permute-start = (bf16[80,64]{0,1:T(8,128)(2,1)S(1)}, bf16[80,64]{0,1:T(8,128)(2,1)S(1)}, u32[]{:S(2)}, u32[]{:S(2)}) collective-permute-start(bf16[80,64]{0,1:T(8,128)(2,1)S(1)} %get-tuple-element.466), channel_id=1, source_target_pairs={{0,64},{64,128},{128,192},{192,256},{256,320},{320,384},{384,448},... | collective-permute-start | bytes 30728 | tf_op jit(solution)/shard_map/while/body/eval_jaxpr/ppermute | solution.py:18
  801.0 0.6 copy-start.1
Sparse Core Ops, SparseCore 0:
  24.8 63.1 reduce-scatter.5
  116.7 58.6 reduce-scatter.5
  204.1 58.9 reduce-scatter.5
  291.4 58.8 reduce-scatter.5
  378.8 58.7 reduce-scatter.5
  465.9 58.9 reduce-scatter.5
  553.2 58.8 reduce-scatter.5
  640.4 58.5 reduce-scatter.5
  727.8 58.1 reduce-scatter.5
where the time goes:
time: 813 us; the launch traced here: 808 us
  waiting for transfers between devices  645 us (79%)
  loops' own time  56.3 us (7%)
  local copies, waits for them, and re-layouts  43.9 us (5%)
  other arithmetic  19.3 us (2%)
  matrix products  18.3 us (2%)
  between operations  13.8 us (2%)
  starting transfers between devices  11.7 us (1%)
    while x18, waiting for transfers between devices  534 us
    ppermute x9, waiting for transfers between devices, passed_along(): return lax.ppermute(block, axis, route)  111 us
    another operation x1, loops' own time, on_device(): lax.fori_loop(0, patches + sections - 1, slot_step, start_state)  56.3 us
    while x72, local copies, waits for them, and re-layouts  17.9 us
    dot_general x9, matrix products, slot_step(): lax.dot_general(local_weight.reshape(9 * local_chan, C), taps, (((0,), (0...  17.5 us
  transfers between devices with their start and end apart: 18, of which 18 were waited for; matrix products, arithmetic and copies ran while one was open for 0% of the time, Pallas kernels for 0%

commit v1 on v0

v1 whole, which is shorter than its diff:
```python
import functools
import math

import jax
import jax.numpy as jnp
from jax import lax
from jax.experimental import pallas as pl
from jax.experimental.pallas import tpu as pltpu
from jax.sharding import PartitionSpec as P

C = 1280
TDIM = 320
W = 32
CELLS = 64
STALE = 4
SECTIONS = 8
Z = 16
BLOCK = 80
HALF = 40
TAPS = 9 * BLOCK
LANES = 128
CHUNKS = ((0, 1, 2, 3), (4, 5, 6, 7), (8, 9, 10, 11), (12, 13, 14, 15))
MESH = pl.DeviceIdType.MESH
F32 = jnp.float32
BF16 = jnp.bfloat16


def step_of(i):
    if i == 0:
        return Z // 2
    distance = Z // 2 - (i + 1) // 2
    return distance if i % 2 else Z - distance


def lane_ids(rows):
    return lax.broadcasted_iota(jnp.int32, (rows, LANES), 1)


def as_column(row):
    square = jnp.broadcast_to(row, (BLOCK, BLOCK))
    diagonal = lax.broadcasted_iota(jnp.int32, (BLOCK, BLOCK), 0) == lax.broadcasted_iota(
        jnp.int32, (BLOCK, BLOCK), 1
    )
    return jnp.sum(jnp.where(diagonal, square, 0.0), axis=1, keepdims=True)


def pack_column(column):
    left = jnp.broadcast_to(column[:HALF], (HALF, LANES))
    right = jnp.broadcast_to(column[HALF:], (HALF, LANES))
    return jnp.where(lane_ids(HALF) < CELLS, left, right)


def pack(block):
    return jnp.where(lane_ids(HALF) < CELLS, block[:HALF], pltpu.roll(block[HALF:], CELLS, 1))


def square_of(rows):
    short_lanes = LANES - rows.shape[1]
    if short_lanes:
        rows = jnp.concatenate([rows, jnp.zeros((rows.shape[0], short_lanes), F32)], axis=1)
    short = LANES - rows.shape[0]
    if short:
        rows = jnp.concatenate([rows, jnp.zeros((short, LANES), F32)], axis=0)
    return rows


def kernel(
    order_ref,
    time_ref,
    step_ref,
    latent_ref,
    stale_ref,
    weight_hbm,
    bias_ref,
    gain_ref,
    shift_ref,
    proj_ref,
    out_ref,
    weight_ref,
    turned_ref,
    gain_packed,
    shift_packed,
    extra_packed,
    halo_ref,
    x_ref,
    recv_ref,
    base_ref,
    send_ref,
    base_out_ref,
    back_ref,
    back_out_ref,
    weight_sem,
    recv_sem,
    base_sem,
    send_sem,
    base_out_sem,
    back_sem,
    back_out_sem,
):
    s = lax.axis_index("section")
    c = lax.axis_index("chan")
    r = lax.axis_index("rep")
    last = SECTIONS - 1
    is_last = s == last
    is_first = s == 0
    kind = jnp.where(is_last, 1, 0)
    target = jnp.where(is_last, last, s + 1)
    behind = jnp.maximum(s - 1, 0)

    weight_copy = pltpu.make_async_copy(weight_hbm, weight_ref, weight_sem)
    weight_copy.start()

    barrier = pltpu.get_barrier_semaphore()

    @pl.when(s > 0)
    def _():
        for i in range(Z):
            z = lax.rem(c + step_of(i) if i < Z - 1 else c, Z)
            pl.semaphore_signal(barrier, inc=1, device_id=(behind, z, r), device_id_type=MESH)

    @pl.when(is_last)
    def _():
        for i in range(Z - 1):
            z = lax.rem(c + step_of(i), Z)
            pl.semaphore_signal(barrier, inc=1, device_id=(s, z, r), device_id_type=MESH)

    @pl.when(s < last)
    def _():
        pl.semaphore_signal(barrier, inc=1, device_id=(s + 1, c, r), device_id_type=MESH)

    first_is_zero = order_ref[0] == 0

    gain_packed[...] = pack_column(as_column(gain_ref[...]))
    shift_packed[...] = pack_column(as_column(shift_ref[...]))

    for p in range(2):
        flat = square_of(latent_ref[p].astype(F32))
        x_ref[p] = pack(jnp.transpose(flat)[:BLOCK])

    below = jnp.zeros((W, BLOCK), F32)
    above = jnp.zeros((W, BLOCK), F32)
    for k in range(STALE):
        below = below + jnp.where(step_ref[0, 1] == k, stale_ref[k, 1, 0].astype(F32), 0.0)
        above = above + jnp.where(step_ref[0, 0] == k, stale_ref[k, 0, 1].astype(F32), 0.0)
    zero_rows = jnp.zeros((2 * W, BLOCK), F32)
    upper = jnp.where(first_is_zero, 0.0, above)
    lower = jnp.where(first_is_zero, below, 0.0)
    halo_ref[...] = jnp.transpose(square_of(jnp.concatenate([upper, zero_rows, lower], axis=0)))[
        :BLOCK
    ]

    weight_copy.wait()

    for j in range(C // LANES):
        turned_ref[pl.ds(LANES * j, LANES), :] = jnp.transpose(
            weight_ref[:, pl.ds(LANES * j, LANES)]
        )

    half = TDIM // 2
    lanes = lax.broadcasted_iota(jnp.int32, (8, TDIM), 1)
    index = jnp.where(lanes < half, lanes, lanes - half).astype(F32)
    angles = time_ref[0].astype(F32) * jnp.exp(index * (-math.log(10000.0) / half))
    emb = jnp.where(lanes < half, jnp.cos(angles), jnp.sin(angles))
    semb = (emb / (1.0 + jnp.exp(-emb))).astype(BF16).astype(F32)
    temb = jnp.sum(proj_ref[...].astype(F32) * semb[:1], axis=1, keepdims=True)
    extra_packed[...] = pack_column(as_column(bias_ref[...]) + temb)

    pl.semaphore_wait(barrier, jnp.where(is_first | is_last, Z, Z + 1))

    wide = lane_ids(BLOCK)
    column = lax.rem(wide, W)
    middle = (wide >= W) & (wide < 3 * W)
    half_lanes = lane_ids(HALF) < CELLS

    def remote(src, dst, send, recv, device):
        return pltpu.make_async_remote_copy(
            src_ref=src,
            dst_ref=dst,
            send_sem=send,
            recv_sem=recv,
            device_id=device,
            device_id_type=MESH,
        )

    def block_copy(q, i):
        return remote(
            send_ref.at[q, i],
            recv_ref.at[kind, q, i],
            send_sem.at[q, i],
            recv_sem.at[kind, q, i],
            (target, lax.rem(c + step_of(i), Z), r),
        )

    def base_copy(q):
        return remote(
            base_out_ref.at[q],
            base_ref.at[q],
            base_out_sem.at[q],
            base_sem.at[q],
            (jnp.minimum(s + 1, last), c, r),
        )

    def back_copy(q):
        return remote(
            back_out_ref.at[q],
            back_ref.at[q],
            back_out_sem.at[q],
            back_sem.at[q],
            (behind, c, r),
        )

    def gathered(which, q, start):
        total = start
        for i in range(Z - 2, -1, -1):
            slot = recv_ref.at[which, q, i]
            pltpu.make_async_copy(slot, slot, recv_sem.at[which, q, i]).wait()
            total = total + recv_ref[which, q, i].astype(F32)
        return total.astype(BF16)

    def group_mean(rows):
        summed = jnp.sum(rows, axis=0, keepdims=True)
        mask = half_lanes[:1]
        left = jnp.sum(jnp.where(mask, summed, 0.0), axis=1, keepdims=True)
        right = jnp.sum(jnp.where(mask, 0.0, summed), axis=1, keepdims=True)
        return jnp.where(mask, left, right) * (1.0 / (HALF * CELLS))

    for q in range(2):
        if q == 0:
            picked = jnp.where(first_is_zero, x_ref[0], x_ref[1])
            other = jnp.where(first_is_zero, x_ref[1], x_ref[0])
            x_ref[0] = picked
            x_ref[1] = other

        @pl.when(s > 0)
        def _():
            base = base_ref.at[q]
            pltpu.make_async_copy(base, base, base_sem.at[q]).wait()
            x_ref[q] = gathered(0, q, base_ref[q]).astype(F32)

        x = x_ref[q]
        mean = group_mean(x)
        centred = x - mean
        variance = group_mean(centred * centred)
        scaled = centred / jnp.sqrt(variance + 1e-05) * gain_packed[...] + shift_packed[...]
        hidden = (scaled / (1.0 + jnp.exp(-scaled))).astype(BF16).astype(F32)
        spread = jnp.concatenate([pltpu.roll(hidden, W, 1), pltpu.roll(hidden, 3 * W, 1)], axis=0)
        halo = halo_ref[...]
        extended = jnp.where(middle, spread, halo)
        if q == 0:
            turned_row = pltpu.roll(extended, CELLS, 1)
            halo_ref[...] = jnp.where(
                first_is_zero,
                jnp.where(wide < W, turned_row, 0.0),
                jnp.where(wide >= 3 * W, turned_row, 0.0),
            )
        shifted = [
            jnp.where(column == 0, 0.0, pltpu.roll(extended, 1, 1)),
            extended,
            jnp.where(column == W - 1, 0.0, pltpu.roll(extended, LANES - 1, 1)),
        ]
        taps = jnp.concatenate(
            [
                (shifted[b] if a == 0 else pltpu.roll(shifted[b], LANES - W * a, 1)).astype(BF16)
                for a in range(3)
                for b in range(3)
            ],
            axis=0,
        )
        for chunk in CHUNKS:
            rows = []
            for i in chunk:
                z = lax.rem(c + step_of(i), Z) if i < Z - 1 else c
                rows.append(turned_ref[pl.ds(pl.multiple_of(z * BLOCK, 16), BLOCK), :])
            product = jnp.dot(jnp.concatenate(rows, axis=0), taps, preferred_element_type=F32)
            for place, i in enumerate(chunk):
                part = pack(product[place * BLOCK : (place + 1) * BLOCK])
                if i < Z - 1:
                    send_ref[q, i] = part.astype(BF16)
                    block_copy(q, i).start()
                else:
                    base_out_ref[q] = x + part + extra_packed[...]

        @pl.when(s < last)
        def _():
            base_copy(q).start()

        @pl.when(s > 0)
        def _():
            back_out_ref[q] = x.astype(BF16)
            back_copy(q).start()

    results = []
    for q in range(2):

        @pl.when(s < last)
        def _():
            back = back_ref.at[q]
            pltpu.make_async_copy(back, back, back_sem.at[q]).wait()
            x_ref[q] = back_ref[q].astype(F32)

        @pl.when(is_last)
        def _():
            x_ref[q] = gathered(1, q, base_out_ref[q]).astype(F32)

        packed = x_ref[q]
        rows = square_of(jnp.concatenate([packed, pltpu.roll(packed, CELLS, 1)], axis=0))
        results.append(jnp.transpose(rows)[:CELLS, :BLOCK].astype(BF16))
    out_ref[0] = jnp.where(first_is_zero, results[0].astype(F32), results[1].astype(F32)).astype(
        BF16
    )
    out_ref[1] = jnp.where(first_is_zero, results[1].astype(F32), results[0].astype(F32)).astype(
        BF16
    )

    for q in range(2):
        for i in range(Z - 1):
            block_copy(q, i).wait_send()

        @pl.when(s < last)
        def _():
            base_copy(q).wait_send()

        @pl.when(s > 0)
        def _():
            back_copy(q).wait_send()


def on_device(
    latent,
    stale_rows,
    conv_weight,
    conv_bias,
    norm_gain,
    norm_shift,
    time_proj,
    patch_order,
    timestep,
    stale_step,
):
    vmem = pl.BlockSpec(memory_space=pltpu.VMEM)
    smem = pl.BlockSpec(memory_space=pltpu.SMEM)
    packed = pltpu.VMEM((HALF, LANES), F32)
    out = pl.pallas_call(
        kernel,
        out_shape=jax.ShapeDtypeStruct((2, CELLS, BLOCK), BF16),
        in_specs=[smem, smem, smem, vmem, vmem, pl.BlockSpec(memory_space=pl.ANY)] + [vmem] * 4,
        out_specs=vmem,
        scratch_shapes=[
            pltpu.VMEM((TAPS, C), BF16),
            pltpu.VMEM((C, TAPS), BF16),
            packed,
            packed,
            packed,
            pltpu.VMEM((BLOCK, LANES), F32),
            pltpu.VMEM((2, HALF, LANES), F32),
            pltpu.VMEM((2, 2, Z - 1, HALF, LANES), BF16),
            pltpu.VMEM((2, HALF, LANES), F32),
            pltpu.VMEM((2, Z - 1, HALF, LANES), BF16),
            pltpu.VMEM((2, HALF, LANES), F32),
            pltpu.VMEM((2, HALF, LANES), BF16),
            pltpu.VMEM((2, HALF, LANES), BF16),
            pltpu.SemaphoreType.DMA,
            pltpu.SemaphoreType.DMA((2, 2, Z - 1)),
            pltpu.SemaphoreType.DMA((2,)),
            pltpu.SemaphoreType.DMA((2, Z - 1)),
            pltpu.SemaphoreType.DMA((2,)),
            pltpu.SemaphoreType.DMA((2,)),
            pltpu.SemaphoreType.DMA((2,)),
        ],
        compiler_params=pltpu.CompilerParams(
            collective_id=0, has_side_effects=True, vmem_limit_bytes=32 * 1024 * 1024
        ),
        name="segments",
    )(
        patch_order,
        timestep,
        stale_step,
        jnp.transpose(latent, (0, 2, 1)),
        jnp.transpose(stale_rows[:, 0], (0, 1, 3, 4, 2)),
        conv_weight.reshape(TAPS, C),
        conv_bias,
        norm_gain,
        norm_shift,
        jnp.transpose(time_proj[0]),
    )
    return jnp.transpose(out, (0, 2, 1))[None]


def solution(mesh):
    placed = (
        P("rep", "chan", None),
        P(None, "section", "rep", "chan", None, None),
        P("section", None, "chan", None),
        P("section", "chan"),
        P("section", "chan"),
        P("section", "chan"),
        P("section", None, "chan"),
        P(),
        P("rep"),
        P("section", None),
    )
    return jax.shard_map(
        on_device,
        mesh=mesh,
        in_specs=placed,
        out_specs=P("section", "rep", "chan", None),
        check_vma=False,
    )
```

time: 813 us -> 93.9 us (0.12)
  waiting for transfers between devices: 645 us -> 0 us
  Pallas kernels: 0 us -> 85.1 us
  loops' own time: 56.3 us -> 0 us
  local copies, waits for them, and re-layouts: 43.9 us -> 7.88 us
  other arithmetic: 19.3 us -> 0 us
  matrix products: 18.3 us -> 0 us
  between operations: 13.8 us -> 0.68 us
  starting transfers between devices: 11.7 us -> 0 us
    while x18 -> x0, waiting for transfers between devices: 534 us -> none
    ppermute x9 -> x0, waiting for transfers between devices: 111 us -> none  [passed_along(): return lax.ppermute(block, axis, route)]
    pallas_call x0 -> x1, Pallas kernels: none -> 85.1 us  [on_device(): pl.pallas_call(kernel, out_shape=jax.ShapeDtypeStruct((2, CELLS, BLOCK),...]
    another operation x1 -> x0, loops' own time: 56.3 us -> none  [on_device(): lax.fori_loop(0, patches + sections - 1, slot_step, start_state)]
    dot_general x10 -> x0, matrix products: 18.3 us -> none  [the longest x9 17.5 us: slot_step(): lax.dot_general(local_weight.reshape(9 * local_chan, C), taps, (((0,), (0...]
    dynamic_slice x27 -> x0, local copies, waits for them, and re-layouts: 18 us -> none  [the longest x9 11.9 us: slot_step(): patch = lax.dynamic_index_in_dim(patch_order, place, 0, keepdims=False)]
    while x72 -> x0, local copies, waits for them, and re-layouts: 17.9 us -> none
    ppermute x9 -> x0, starting transfers between devices: 11.6 us -> none  [passed_along(): return lax.ppermute(block, axis, route)]
  transfers between devices with their start and end apart: 18 -> 0, of which waited for: 18 -> 0; matrix products, arithmetic and copies ran while one was open for 0% -> 0% of each run, Pallas kernels for 0% -> 0%
where the time goes in v1:
time: 93.9 us; the launch traced here: 93.6 us
  Pallas kernels  85.1 us (91%)
  local copies, waits for them, and re-layouts  7.88 us (8%)
    pallas_call x1, Pallas kernels, on_device(): pl.pallas_call(kernel, out_shape=jax.ShapeDtypeStruct((2, CELLS, BLOCK),...  85.1 us
    unnamed x19, local copies, waits for them, and re-layouts  7.88 us

profile of v1, /device:TPU:25, one launch (start us, length us, event | category | flops | bytes accessed | tf_op | source)
XLA Modules:
  0.0 93.6 jit_solution(17891800374784536975)
XLA Ops:
  0.7 0.0 copy-start
  0.7 1.5 %copy-done = bf16[1,9,80,1280]{3,2,1,0:T(8,128)(2,1)S(1)} copy-done((bf16[1,9,80,1280]{3,2,1,0:T(8,128)(2,1)S(1)}, bf16[1,9,80,1280]{3,2,1,0:T(8,128)(2,1)}, u32[]{:S(2)}) %copy-start) | copy-done | bytes 1843224
  2.2 0.0 copy-start.1
  2.2 0.9 copy-done.1
  3.1 0.0 copy-start.2
  3.1 0.8 copy-done.2
  3.9 0.0 copy-start.3
  3.9 0.8 copy-done.3
  4.6 0.0 copy-start.4
  4.7 0.7 copy-done.4
  5.3 0.0 copy-start.5
  5.3 0.7 copy-done.5
  6.0 0.0 copy-start.6
  6.0 0.7 copy-done.6
  6.6 0.0 copy-start.7
  6.6 0.7 copy-done.7
  7.3 0.0 copy-start.8
  7.3 0.7 copy-done.8
  7.9 85.1 %segments.1 = bf16[2,64,80]{2,1,0:T(8,128)(2,1)S(1)} custom-call(s32[2]{0:T(128)S(1)} %copy-done.4, s32[1]{0:T(128)S(6)} %copy.12.time_ref, s32[1,2]{1,0:T(1,128)S(1)} %copy-done.5, bf16[2,64,80]{2,1,0:T(8,128)(2,1)S(1)} %bitcast.15, bf16[4,2,2,32,80]{4,3,2,1,0:T(8,128)(2,1)S(1)} %bitcast.13, bf16[720,1280]{1,0:T(8,128)(2,1)S(1)} %bitcast.11, ...), custom_call_target="tpu_custom_call" | custom-call | tf_op jit(solution)/shard_map/segments/pallas_call | solution.py:343
  93.0 0.6 copy.13
Async XLA Ops:
  0.7 1.5 %copy-start = (bf16[1,9,80,1280]{3,2,1,0:T(8,128)(2,1)S(1)}, bf16[1,9,80,1280]{3,2,1,0:T(8,128)(2,1)}, u32[]{:S(2)}) copy-start(bf16[1,9,80,1280]{3,2,1,0:T(8,128)(2,1)} %param.12) | copy-start | bytes 5529604
  2.2 0.9 copy-start.1
  3.1 0.8 copy-start.2
  3.9 0.8 copy-start.3
  4.6 0.7 copy-start.4
  5.3 0.7 copy-start.5
  6.0 0.7 copy-start.6
  6.6 0.7 copy-start.7
  7.3 0.7 copy-start.8

commit v2 on v1

--- a/solution.py
+++ b/solution.py
@@ -17,9 +17,14 @@
 Z = 16
 BLOCK = 80
 HALF = 40
+PIECE = 256
 TAPS = 9 * BLOCK
 LANES = 128
-CHUNKS = ((0, 1, 2, 3), (4, 5, 6, 7), (8, 9, 10, 11), (12, 13, 14, 15))
+OWN = Z - 1
+FAR_CHUNKS = ((0,), (1, 2), (3, 4, 5, 6))
+MIDDLE_CHUNKS = ((7, 8), (9, 10))
+NEAR_CHUNK = (11, 12, 13, 14)
+FAR = 7
 MESH = pl.DeviceIdType.MESH
 F32 = jnp.float32
 BF16 = jnp.bfloat16
@@ -65,17 +70,27 @@
 
 
 def kernel(
+    order_hbm,
+    time_hbm,
+    step_hbm,
+    latent_hbm,
+    stale_hbm,
+    weight_hbm,
+    bias_hbm,
+    gain_hbm,
+    shift_hbm,
+    proj_hbm,
+    out_ref,
     order_ref,
     time_ref,
     step_ref,
     latent_ref,
-    stale_ref,
-    weight_hbm,
+    below_ref,
+    above_ref,
     bias_ref,
     gain_ref,
     shift_ref,
     proj_ref,
-    out_ref,
     weight_ref,
     turned_ref,
     gain_packed,
@@ -90,6 +105,7 @@
     back_ref,
     back_out_ref,
     weight_sem,
+    load_sem,
     recv_sem,
     base_sem,
     send_sem,
@@ -107,8 +123,31 @@
     target = jnp.where(is_last, last, s + 1)
     behind = jnp.maximum(s - 1, 0)
 
-    weight_copy = pltpu.make_async_copy(weight_hbm, weight_ref, weight_sem)
-    weight_copy.start()
+    loads = [
+        pltpu.make_async_copy(src, dst, load_sem.at[i])
+        for i, (src, dst) in enumerate(
+            (
+                (latent_hbm, latent_ref),
+                (order_hbm, order_ref),
+                (gain_hbm, gain_ref),
+                (shift_hbm, shift_ref),
+                (step_hbm, step_ref),
+                (stale_hbm.at[:, 1, 0], below_ref),
+                (stale_hbm.at[:, 0, 1], above_ref),
+                (time_hbm, time_ref),
+                (bias_hbm, bias_ref),
+                (proj_hbm, proj_ref),
+            )
+        )
+    ]
+    weight_copies = [
+        pltpu.make_async_copy(
+            weight_hbm.at[:, pl.ds(PIECE * j, PIECE)],
+            weight_ref.at[:, pl.ds(PIECE * j, PIECE)],
+            weight_sem.at[j],
+        )
+        for j in range(C // PIECE)
+    ]
 
     barrier = pltpu.get_barrier_semaphore()
 
@@ -128,33 +167,58 @@
     def _():
         pl.semaphore_signal(barrier, inc=1, device_id=(s + 1, c, r), device_id_type=MESH)
 
+    for load in loads[:7]:
+        load.start()
+    for copy in weight_copies:
+        copy.start()
+    for load in loads[7:]:
+        load.start()
+
+    for load in loads[:7]:
+        load.wait()
     first_is_zero = order_ref[0] == 0
 
     gain_packed[...] = pack_column(as_column(gain_ref[...]))
     shift_packed[...] = pack_column(as_column(shift_ref[...]))
 
-    for p in range(2):
-        flat = square_of(latent_ref[p].astype(F32))
-        x_ref[p] = pack(jnp.transpose(flat)[:BLOCK])
+    @pl.when(is_first)
+    def _():
+        packed = [pack(jnp.transpose(square_of(latent_ref[p].astype(F32)))[:BLOCK]) for p in (0, 1)]
+        x_ref[0] = jnp.where(first_is_zero, packed[0], packed[1])
+        x_ref[1] = jnp.where(first_is_zero, packed[1], packed[0])
 
     below = jnp.zeros((W, BLOCK), F32)
     above = jnp.zeros((W, BLOCK), F32)
     for k in range(STALE):
-        below = below + jnp.where(step_ref[0, 1] == k, stale_ref[k, 1, 0].astype(F32), 0.0)
-        above = above + jnp.where(step_ref[0, 0] == k, stale_ref[k, 0, 1].astype(F32), 0.0)
+        below = below + jnp.where(step_ref[0, 1] == k, below_ref[k].astype(F32), 0.0)
+        above = above + jnp.where(step_ref[0, 0] == k, above_ref[k].astype(F32), 0.0)
     zero_rows = jnp.zeros((2 * W, BLOCK), F32)
     upper = jnp.where(first_is_zero, 0.0, above)
     lower = jnp.where(first_is_zero, below, 0.0)
-    halo_ref[...] = jnp.transpose(square_of(jnp.concatenate([upper, zero_rows, lower], axis=0)))[
-        :BLOCK
-    ]
-
-    weight_copy.wait()
-
-    for j in range(C // LANES):
-        turned_ref[pl.ds(LANES * j, LANES), :] = jnp.transpose(
-            weight_ref[:, pl.ds(LANES * j, LANES)]
-        )
+    wide = lane_ids(BLOCK)
+    column = lax.rem(wide, W)
+    half_lanes = lane_ids(HALF) < CELLS
+
+    def set_halo(halo):
+        for b in range(3):
+            moved = halo
+            if b != 1:
+                edge = 0 if b == 0 else W - 1
+                moved = jnp.where(column == edge, 0.0, pltpu.roll(halo, (1 - b) % LANES, 1))
+            for a in (0, 2):
+                halo_ref[3 * a + b] = moved if a == 0 else pltpu.roll(moved, CELLS, 1)
+
+    set_halo(
+        jnp.transpose(square_of(jnp.concatenate([upper, zero_rows, lower], axis=0)))[:BLOCK]
+    )
+
+    for j in range(C // PIECE):
+        weight_copies[j].wait()
+        turned_ref[pl.ds(PIECE * j, PIECE), :] = jnp.transpose(
+            weight_ref[:, pl.ds(PIECE * j, PIECE)]
+        )
+    for load in loads[7:]:
+        load.wait()
 
     half = TDIM // 2
     lanes = lax.broadcasted_iota(jnp.int32, (8, TDIM), 1)
@@ -165,13 +229,6 @@
     temb = jnp.sum(proj_ref[...].astype(F32) * semb[:1], axis=1, keepdims=True)
     extra_packed[...] = pack_column(as_column(bias_ref[...]) + temb)
 
-    pl.semaphore_wait(barrier, jnp.where(is_first | is_last, Z, Z + 1))
-
-    wide = lane_ids(BLOCK)
-    column = lax.rem(wide, W)
-    middle = (wide >= W) & (wide < 3 * W)
-    half_lanes = lane_ids(HALF) < CELLS
-
     def remote(src, dst, send, recv, device):
         return pltpu.make_async_remote_copy(
             src_ref=src,
@@ -224,70 +281,113 @@
         right = jnp.sum(jnp.where(mask, 0.0, summed), axis=1, keepdims=True)
         return jnp.where(mask, left, right) * (1.0 / (HALF * CELLS))
 
-    for q in range(2):
-        if q == 0:
-            picked = jnp.where(first_is_zero, x_ref[0], x_ref[1])
-            other = jnp.where(first_is_zero, x_ref[1], x_ref[0])
-            x_ref[0] = picked
-            x_ref[1] = other
-
-        @pl.when(s > 0)
-        def _():
-            base = base_ref.at[q]
-            pltpu.make_async_copy(base, base, base_sem.at[q]).wait()
-            x_ref[q] = gathered(0, q, base_ref[q]).astype(F32)
-
-        x = x_ref[q]
+    def taps_of(q, x):
         mean = group_mean(x)
         centred = x - mean
         variance = group_mean(centred * centred)
-        scaled = centred / jnp.sqrt(variance + 1e-05) * gain_packed[...] + shift_packed[...]
-        hidden = (scaled / (1.0 + jnp.exp(-scaled))).astype(BF16).astype(F32)
+        scaled = centred * (1.0 / jnp.sqrt(variance + 1e-05)) * gain_packed[...] + shift_packed[...]
+        hidden = scaled / (1.0 + jnp.exp(-scaled))
+        taps = []
+        for a in range(3):
+            for b in range(3):
+                shift = W * (a - 1) + b - 1
+                moved = jnp.concatenate(
+                    [
+                        pltpu.roll(hidden, -shift % LANES, 1) if shift else hidden,
+                        pltpu.roll(hidden, (CELLS - shift) % LANES, 1),
+                    ],
+                    axis=0,
+                )
+                valid = None
+                if a != 1:
+                    valid = wide >= W if a == 0 else wide < W
+                if b != 1:
+                    inside = column != (0 if b == 0 else W - 1)
+                    valid = inside if valid is None else valid & inside
+                if valid is not None:
+                    moved = jnp.where(valid, moved, 0.0 if a == 1 else halo_ref[3 * a + b])
+                taps.append(moved.astype(BF16))
+        return hidden, jnp.concatenate(taps, axis=0)
+
+    def next_halo(hidden):
         spread = jnp.concatenate([pltpu.roll(hidden, W, 1), pltpu.roll(hidden, 3 * W, 1)], axis=0)
-        halo = halo_ref[...]
-        extended = jnp.where(middle, spread, halo)
-        if q == 0:
-            turned_row = pltpu.roll(extended, CELLS, 1)
-            halo_ref[...] = jnp.where(
+        turned_row = pltpu.roll(spread, CELLS, 1)
+        set_halo(
+            jnp.where(
                 first_is_zero,
                 jnp.where(wide < W, turned_row, 0.0),
                 jnp.where(wide >= 3 * W, turned_row, 0.0),
             )
-        shifted = [
-            jnp.where(column == 0, 0.0, pltpu.roll(extended, 1, 1)),
-            extended,
-            jnp.where(column == W - 1, 0.0, pltpu.roll(extended, LANES - 1, 1)),
-        ]
-        taps = jnp.concatenate(
-            [
-                (shifted[b] if a == 0 else pltpu.roll(shifted[b], LANES - W * a, 1)).astype(BF16)
-                for a in range(3)
-                for b in range(3)
-            ],
-            axis=0,
-        )
-        for chunk in CHUNKS:
-            rows = []
-            for i in chunk:
-                z = lax.rem(c + step_of(i), Z) if i < Z - 1 else c
-                rows.append(turned_ref[pl.ds(pl.multiple_of(z * BLOCK, 16), BLOCK), :])
-            product = jnp.dot(jnp.concatenate(rows, axis=0), taps, preferred_element_type=F32)
-            for place, i in enumerate(chunk):
-                part = pack(product[place * BLOCK : (place + 1) * BLOCK])
-                if i < Z - 1:
-                    send_ref[q, i] = part.astype(BF16)
-                    block_copy(q, i).start()
-                else:
-                    base_out_ref[q] = x + part + extra_packed[...]
-
-        @pl.when(s < last)
-        def _():
+        )
+
+    def multiply(q, taps, chunk):
+        rows = []
+        for i in chunk:
+            z = c if i == OWN else lax.rem(c + step_of(i), Z)
+            rows.append(turned_ref[pl.ds(pl.multiple_of(z * BLOCK, 16), BLOCK), :])
+        product = jnp.dot(jnp.concatenate(rows, axis=0), taps, preferred_element_type=F32)
+        parts = [pack(product[k * BLOCK : (k + 1) * BLOCK]) for k in range(len(chunk))]
+        for i, part in zip(chunk, parts):
+            if i != OWN:
+                send_ref[q, i] = part.astype(BF16)
+        return parts
+
+    def start(q, chunk):
+        for i in chunk:
+            block_copy(q, i).start()
+
+    def finish(q):
+        for i in range(FAR):
+            block_copy(q, i).wait_send()
+        start(q, NEAR_CHUNK)
+
+    @pl.when(is_first)
+    def _():
+        for q in range(2):
+            x = x_ref[q]
+            hidden, taps = taps_of(q, x)
+            for chunk in FAR_CHUNKS + MIDDLE_CHUNKS + (NEAR_CHUNK,):
+                multiply(q, taps, chunk)
+            base_out_ref[q] = x + multiply(q, taps, (OWN,))[0] + extra_packed[...]
+            if q == 0:
+                next_halo(hidden)
+
+    pl.semaphore_wait(barrier, jnp.where(is_first | is_last, Z, Z + 1))
+
+    @pl.when(is_first)
+    def _():
+        for q in range(2):
+            for chunk in FAR_CHUNKS + MIDDLE_CHUNKS:
+                start(q, chunk)
             base_copy(q).start()
-
-        @pl.when(s > 0)
-        def _():
+            finish(q)
+
+    @pl.when(s > 0)
+    def _():
+        for q in range(2):
+            base = base_ref.at[q]
+            pltpu.make_async_copy(base, base, base_sem.at[q]).wait()
+            x = gathered(0, q, base_ref[q]).astype(F32)
+            hidden, taps = taps_of(q, x)
+            for chunk in FAR_CHUNKS:
+                multiply(q, taps, chunk)
+                start(q, chunk)
+            multiply(q, taps, MIDDLE_CHUNKS[0])
+            start(q, MIDDLE_CHUNKS[0])
+            base_out_ref[q] = x + multiply(q, taps, (OWN,))[0] + extra_packed[...]
+
+            @pl.when(s < last)
+            def _():
+                base_copy(q).start()
+
+            multiply(q, taps, MIDDLE_CHUNKS[1])
+            start(q, MIDDLE_CHUNKS[1])
             back_out_ref[q] = x.astype(BF16)
             back_copy(q).start()
+            multiply(q, taps, NEAR_CHUNK)
+            if q == 0:
+                next_halo(hidden)
+            finish(q)
 
     results = []
     for q in range(2):
@@ -313,7 +413,7 @@
     )
 
     for q in range(2):
-        for i in range(Z - 1):
+        for i in range(FAR, Z - 1):
             block_copy(q, i).wait_send()
 
         @pl.when(s < last)
@@ -337,21 +437,29 @@
     timestep,
     stale_step,
 ):
-    vmem = pl.BlockSpec(memory_space=pltpu.VMEM)
-    smem = pl.BlockSpec(memory_space=pltpu.SMEM)
     packed = pltpu.VMEM((HALF, LANES), F32)
     out = pl.pallas_call(
         kernel,
-        out_shape=jax.ShapeDtypeStruct((2, CELLS, BLOCK), BF16),
-        in_specs=[smem, smem, smem, vmem, vmem, pl.BlockSpec(memory_space=pl.ANY)] + [vmem] * 4,
-        out_specs=vmem,
+        out_shape=pltpu.VMEM((2, CELLS, BLOCK), BF16),
+        in_specs=[pl.BlockSpec(memory_space=pltpu.HBM)] * 10,
+        out_specs=pl.BlockSpec(memory_space=pltpu.VMEM),
         scratch_shapes=[
+            pltpu.SMEM((2,), jnp.int32),
+            pltpu.SMEM((1,), jnp.int32),
+            pltpu.SMEM((1, 2), jnp.int32),
+            pltpu.VMEM((2, CELLS, BLOCK), BF16),
+            pltpu.VMEM((STALE, W, BLOCK), BF16),
+            pltpu.VMEM((STALE, W, BLOCK), BF16),
+            pltpu.VMEM((1, BLOCK), F32),
+            pltpu.VMEM((1, BLOCK), F32),
+            pltpu.VMEM((1, BLOCK), F32),
+            pltpu.VMEM((BLOCK, TDIM), BF16),
             pltpu.VMEM((TAPS, C), BF16),
             pltpu.VMEM((C, TAPS), BF16),
             packed,
             packed,
             packed,
-            pltpu.VMEM((BLOCK, LANES), F32),
+            pltpu.VMEM((9, BLOCK, LANES), F32),
             pltpu.VMEM((2, HALF, LANES), F32),
             pltpu.VMEM((2, 2, Z - 1, HALF, LANES), BF16),
             pltpu.VMEM((2, HALF, LANES), F32),
@@ -359,7 +467,8 @@
             pltpu.VMEM((2, HALF, LANES), F32),
             pltpu.VMEM((2, HALF, LANES), BF16),
             pltpu.VMEM((2, HALF, LANES), BF16),
-            pltpu.SemaphoreType.DMA,
+            pltpu.SemaphoreType.DMA((C // PIECE,)),
+            pltpu.SemaphoreType.DMA((10,)),
             pltpu.SemaphoreType.DMA((2, 2, Z - 1)),
             pltpu.SemaphoreType.DMA((2,)),
             pltpu.SemaphoreType.DMA((2, Z - 1)),
@@ -368,7 +477,7 @@
             pltpu.SemaphoreType.DMA((2,)),
         ],
         compiler_params=pltpu.CompilerParams(
-            collective_id=0, has_side_effects=True, vmem_limit_bytes=32 * 1024 * 1024
+            collective_id=0, has_side_effects=True, vmem_limit_bytes=60 * 1024 * 1024
         ),
         name="segments",
     )(

time: 93.9 us -> 87.2 us (0.929)
  local copies, waits for them, and re-layouts: 7.88 us -> 0.62 us
    unnamed x19 -> x1, local copies, waits for them, and re-layouts: 7.88 us -> 0.62 us
where the time goes in v2:
time: 87.2 us; the launch traced here: 86.2 us
  Pallas kernels  84.9 us (97%)
    pallas_call x1, Pallas kernels, on_device(): pl.pallas_call(kernel, out_shape=pltpu.VMEM((2, CELLS, BLOCK), BF16), in_...  84.9 us

profile of v2, /device:TPU:25, one launch (start us, length us, event | category | flops | bytes accessed | tf_op | source)
XLA Modules:
  0.0 86.2 jit_solution(13853000780248577022)
XLA Ops:
  0.7 84.9 %segments.1 = bf16[2,64,80]{2,1,0:T(8,128)(2,1)S(1)} custom-call(s32[2]{0:T(128)} %order_hbm.1, s32[1]{0:T(128)S(6)} %copy.13.time_hbm, s32[1,2]{1,0:T(1,128)} %step_hbm.1, bf16[2,64,80]{2,1,0:T(8,128)(2,1)} %bitcast.15, bf16[4,2,2,32,80]{4,3,2,1,0:T(8,128)(2,1)} %bitcast.13, bf16[720,1280]{1,0:T(8,128)(2,1)} %bitcast.12, f32[1,80]{1,0:T(1,128)} %bias_hbm.1, ...), custom_call_target="tpu_custom_call" | custom-call | tf_op jit(solution)/shard_map/segments/pallas_call | solution.py:441
  85.5 0.6 copy.12

commit v3 on v2

--- a/solution.py
+++ b/solution.py
@@ -25,6 +25,7 @@
 MIDDLE_CHUNKS = ((7, 8), (9, 10))
 NEAR_CHUNK = (11, 12, 13, 14)
 FAR = 7
+PAUSE = 6
 MESH = pl.DeviceIdType.MESH
 F32 = jnp.float32
 BF16 = jnp.bfloat16
@@ -35,6 +36,20 @@
         return Z // 2
     distance = Z // 2 - (i + 1) // 2
     return distance if i % 2 else Z - distance
+
+
+def odd(z):
+    return lax.rem(z, 2) == 1
+
+
+def holder(t, z):
+    moved = jnp.where(t < 6, t + 2, t - 2)
+    return jnp.where(odd(z) & (t >= 4), moved, t)
+
+
+def section_of(s, z):
+    taken = jnp.where(s < 6, s + 2, s - 2)
+    return jnp.where(odd(z) & (s >= 4), taken, s)
 
 
 def lane_ids(rows):
@@ -93,9 +108,10 @@
     proj_ref,
     weight_ref,
     turned_ref,
-    gain_packed,
-    shift_packed,
-    extra_packed,
+    own_packed,
+    packed_ref,
+    own_halo,
+    given_halo,
     halo_ref,
     x_ref,
     recv_ref,
@@ -106,6 +122,11 @@
     back_out_ref,
     weight_sem,
     load_sem,
+    move_out_sem,
+    move_sem,
+    pass_out_sem,
+    pass_sem,
+    turn_sem,
     recv_sem,
     base_sem,
     send_sem,
@@ -117,11 +138,19 @@
     c = lax.axis_index("chan")
     r = lax.axis_index("rep")
     last = SECTIONS - 1
-    is_last = s == last
     is_first = s == 0
-    kind = jnp.where(is_last, 1, 0)
-    target = jnp.where(is_last, last, s + 1)
-    behind = jnp.maximum(s - 1, 0)
+    role = section_of(s, c)
+    host = holder(s, c)
+    swapped = role != s
+    core = lax.rem(s, 2)
+    ends = role == last
+    stays = ends & (s == last)
+    kind = jnp.where(ends, 1, 0)
+    ahead = jnp.minimum(role + 1, last)
+    behind = jnp.maximum(role - 1, 0)
+
+    def target(z):
+        return jnp.where(ends, last, holder(ahead, z))
 
     loads = [
         pltpu.make_async_copy(src, dst, load_sem.at[i])
@@ -140,37 +169,52 @@
             )
         )
     ]
-    weight_copies = [
-        pltpu.make_async_copy(
-            weight_hbm.at[:, pl.ds(PIECE * j, PIECE)],
-            weight_ref.at[:, pl.ds(PIECE * j, PIECE)],
-            weight_sem.at[j],
-        )
-        for j in range(C // PIECE)
-    ]
+    weight_copy = pltpu.make_async_copy(weight_hbm, weight_ref, weight_sem)
+
+    def greet(section, z):
+        pl.semaphore_signal(barrier, inc=1, device_id=(section, z, r), device_id_type=MESH)
 
     barrier = pltpu.get_barrier_semaphore()
 
-    @pl.when(s > 0)
+    @pl.when(role > 0)
     def _():
         for i in range(Z):
-            z = lax.rem(c + step_of(i) if i < Z - 1 else c, Z)
-            pl.semaphore_signal(barrier, inc=1, device_id=(behind, z, r), device_id_type=MESH)
-
-    @pl.when(is_last)
+            z = lax.rem(c + step_of(i), Z) if i < OWN else c
+            greet(holder(behind, z), z)
+
+    @pl.when(s == last)
     def _():
         for i in range(Z - 1):
             z = lax.rem(c + step_of(i), Z)
-            pl.semaphore_signal(barrier, inc=1, device_id=(s, z, r), device_id_type=MESH)
+            greet(holder(last, z), z)
+
+    @pl.when((s == last) & swapped)
+    def _():
+        greet(holder(last, c), c)
 
     @pl.when(s < last)
     def _():
-        pl.semaphore_signal(barrier, inc=1, device_id=(s + 1, c, r), device_id_type=MESH)
+        greet(holder(s + 1, c), c)
+
+    @pl.when(swapped)
+    def _():
+        greet(role, c)
+        for i in range(1, 4):
+            pl.semaphore_signal(
+                barrier, inc=1, device_id=(s, c, lax.rem(r + i, 4)), device_id_type=MESH
+            )
+
+    @pl.when(swapped & (core == 1))
+    def _():
+        greet(s - 1, c)
 
     for load in loads[:7]:
         load.start()
-    for copy in weight_copies:
-        copy.start()
+
+    @pl.when(jnp.logical_not(swapped))
+    def _():
+        weight_copy.start()
+
     for load in loads[7:]:
         load.start()
 
@@ -178,8 +222,8 @@
         load.wait()
     first_is_zero = order_ref[0] == 0
 
-    gain_packed[...] = pack_column(as_column(gain_ref[...]))
-    shift_packed[...] = pack_column(as_column(shift_ref[...]))
+    own_packed[0] = pack_column(as_column(gain_ref[...]))
+    own_packed[1] = pack_column(as_column(shift_ref[...]))
 
     @pl.when(is_first)
     def _():
@@ -208,15 +252,10 @@
             for a in (0, 2):
                 halo_ref[3 * a + b] = moved if a == 0 else pltpu.roll(moved, CELLS, 1)
 
-    set_halo(
-        jnp.transpose(square_of(jnp.concatenate([upper, zero_rows, lower], axis=0)))[:BLOCK]
-    )
-
-    for j in range(C // PIECE):
-        weight_copies[j].wait()
-        turned_ref[pl.ds(PIECE * j, PIECE), :] = jnp.transpose(
-            weight_ref[:, pl.ds(PIECE * j, PIECE)]
-        )
+    own_halo[...] = jnp.transpose(
+        square_of(jnp.concatenate([upper, zero_rows, lower], axis=0))
+    )[:BLOCK]
+
     for load in loads[7:]:
         load.wait()
 
@@ -227,7 +266,20 @@
     emb = jnp.where(lanes < half, jnp.cos(angles), jnp.sin(angles))
     semb = (emb / (1.0 + jnp.exp(-emb))).astype(BF16).astype(F32)
     temb = jnp.sum(proj_ref[...].astype(F32) * semb[:1], axis=1, keepdims=True)
-    extra_packed[...] = pack_column(as_column(bias_ref[...]) + temb)
+    own_packed[2] = pack_column(as_column(bias_ref[...]) + temb)
+
+    def turn():
+        for j in range(C // PIECE):
+            turned_ref[pl.ds(PIECE * j, PIECE), :] = jnp.transpose(
+                weight_ref[:, :, pl.ds(PIECE * j, PIECE)].reshape(TAPS, PIECE)
+            )
+
+    @pl.when(jnp.logical_not(swapped))
+    def _():
+        packed_ref[...] = own_packed[...]
+        set_halo(own_halo[...])
+        weight_copy.wait()
+        turn()
 
     def remote(src, dst, send, recv, device):
         return pltpu.make_async_remote_copy(
@@ -245,16 +297,16 @@
             recv_ref.at[kind, q, i],
             send_sem.at[q, i],
             recv_sem.at[kind, q, i],
-            (target, lax.rem(c + step_of(i), Z), r),
+            (target(lax.rem(c + step_of(i), Z)), lax.rem(c + step_of(i), Z), r),
         )
 
     def base_copy(q):
         return remote(
             base_out_ref.at[q],
-            base_ref.at[q],
+            base_ref.at[kind, q],
             base_out_sem.at[q],
-            base_sem.at[q],
-            (jnp.minimum(s + 1, last), c, r),
+            base_sem.at[kind, q],
+            (target(c), c, r),
         )
 
     def back_copy(q):
@@ -266,9 +318,10 @@
             (behind, c, r),
         )
 
-    def gathered(which, q, start):
-        total = start
+    def gathered(which, q, total, between=None):
         for i in range(Z - 2, -1, -1):
+            if between is not None and i == PAUSE:
+                between()
             slot = recv_ref.at[which, q, i]
             pltpu.make_async_copy(slot, slot, recv_sem.at[which, q, i]).wait()
             total = total + recv_ref[which, q, i].astype(F32)
@@ -285,7 +338,7 @@
         mean = group_mean(x)
         centred = x - mean
         variance = group_mean(centred * centred)
-        scaled = centred * (1.0 / jnp.sqrt(variance + 1e-05)) * gain_packed[...] + shift_packed[...]
+        scaled = centred * (1.0 / jnp.sqrt(variance + 1e-05)) * packed_ref[0] + packed_ref[1]
         hidden = scaled / (1.0 + jnp.exp(-scaled))
         taps = []
         for a in range(3):
@@ -348,11 +401,65 @@
             hidden, taps = taps_of(q, x)
             for chunk in FAR_CHUNKS + MIDDLE_CHUNKS + (NEAR_CHUNK,):
                 multiply(q, taps, chunk)
-            base_out_ref[q] = x + multiply(q, taps, (OWN,))[0] + extra_packed[...]
+            base_out_ref[q] = x + multiply(q, taps, (OWN,))[0] + packed_ref[2]
             if q == 0:
                 next_halo(hidden)
 
-    pl.semaphore_wait(barrier, jnp.where(is_first | is_last, Z, Z + 1))
+    greeted = jnp.where(stays, Z - 1, Z) + jnp.where(role > 0, 1, 0)
+    greeted = greeted + jnp.where(swapped, jnp.where(core == 0, 5, 4), 0)
+    pl.semaphore_wait(barrier, greeted)
+
+    @pl.when(swapped)
+    def _():
+        moves = [
+            remote(src, dst, move_out_sem.at[i], move_sem.at[i], (host, c, r))
+            for i, (src, dst) in enumerate(
+                (
+                    (weight_hbm.at[2 * r], weight_ref.at[2 * r]),
+                    (weight_hbm.at[2 * r + 1], weight_ref.at[2 * r + 1]),
+                    (weight_hbm.at[8], weight_ref.at[8]),
+                    (own_packed, packed_ref),
+                    (own_halo, given_halo),
+                )
+            )
+        ]
+
+        @pl.when(core == 1)
+        def _():
+            pl.semaphore_wait(turn_sem, 1)
+
+        for copy in moves:
+            copy.start()
+
+        def passed(i, j):
+            return remote(
+                weight_ref.at[2 * r + j],
+                weight_ref.at[2 * r + j],
+                pass_out_sem.at[i - 1, j],
+                pass_sem.at[i - 1, j],
+                (s, c, lax.rem(r + i, 4)),
+            )
+
+        for j in range(2):
+            moves[j].wait_recv()
+            for i in (2, 1, 3):
+                passed(i, j).start()
+        for copy in moves:
+            copy.wait_send()
+
+        @pl.when(core == 0)
+        def _():
+            pl.semaphore_signal(turn_sem, inc=1, device_id=(s + 1, c, r), device_id_type=MESH)
+
+        for copy in moves[2:]:
+            copy.wait_recv()
+        set_halo(given_halo[...])
+        for j in range(2):
+            for i in range(1, 4):
+                passed(i, j).wait_send()
+                slot = weight_ref.at[2 * lax.rem(r + 4 - i, 4) + j]
+                pltpu.make_async_copy(slot, slot, pass_sem.at[i - 1, j]).wait()
+        turn()
 
     @pl.when(is_first)
     def _():
@@ -365,18 +472,19 @@
     @pl.when(s > 0)
     def _():
         for q in range(2):
-            base = base_ref.at[q]
-            pltpu.make_async_copy(base, base, base_sem.at[q]).wait()
-            x = gathered(0, q, base_ref[q]).astype(F32)
+            base = base_ref.at[0, q]
+            pltpu.make_async_copy(base, base, base_sem.at[0, q]).wait()
+            near = functools.partial(start, 0, NEAR_CHUNK) if q else None
+            x = gathered(0, q, base_ref[0, q], near).astype(F32)
             hidden, taps = taps_of(q, x)
             for chunk in FAR_CHUNKS:
                 multiply(q, taps, chunk)
                 start(q, chunk)
             multiply(q, taps, MIDDLE_CHUNKS[0])
             start(q, MIDDLE_CHUNKS[0])
-            base_out_ref[q] = x + multiply(q, taps, (OWN,))[0] + extra_packed[...]
-
-            @pl.when(s < last)
+            base_out_ref[q] = x + multiply(q, taps, (OWN,))[0] + packed_ref[2]
+
+            @pl.when(jnp.logical_not(stays))
             def _():
                 base_copy(q).start()
 
@@ -387,7 +495,8 @@
             multiply(q, taps, NEAR_CHUNK)
             if q == 0:
                 next_halo(hidden)
-            finish(q)
+            else:
+                finish(q)
 
     results = []
     for q in range(2):
@@ -398,9 +507,19 @@
             pltpu.make_async_copy(back, back, back_sem.at[q]).wait()
             x_ref[q] = back_ref[q].astype(F32)
 
-        @pl.when(is_last)
-        def _():
-            x_ref[q] = gathered(1, q, base_out_ref[q]).astype(F32)
+        @pl.when(stays)
+        def _():
+            x_ref[q] = base_out_ref[q]
+
+        @pl.when((s == last) & jnp.logical_not(stays))
+        def _():
+            base = base_ref.at[1, q]
+            pltpu.make_async_copy(base, base, base_sem.at[1, q]).wait()
+            x_ref[q] = base_ref[1, q]
+
+        @pl.when(s == last)
+        def _():
+            x_ref[q] = gathered(1, q, x_ref[q]).astype(F32)
 
         packed = x_ref[q]
         rows = square_of(jnp.concatenate([packed, pltpu.roll(packed, CELLS, 1)], axis=0))
@@ -415,8 +534,14 @@
     for q in range(2):
         for i in range(FAR, Z - 1):
             block_copy(q, i).wait_send()
-
-        @pl.when(s < last)
+        if q == 0:
+
+            @pl.when(s > 0)
+            def _():
+                for i in range(FAR):
+                    block_copy(0, i).wait_send()
+
+        @pl.when(jnp.logical_not(stays))
         def _():
             base_copy(q).wait_send()
 
@@ -437,7 +562,6 @@
     timestep,
     stale_step,
 ):
-    packed = pltpu.VMEM((HALF, LANES), F32)
     out = pl.pallas_call(
         kernel,
         out_shape=pltpu.VMEM((2, CELLS, BLOCK), BF16),
@@ -454,23 +578,29 @@
             pltpu.VMEM((1, BLOCK), F32),
             pltpu.VMEM((1, BLOCK), F32),
             pltpu.VMEM((BLOCK, TDIM), BF16),
-            pltpu.VMEM((TAPS, C), BF16),
+            pltpu.VMEM((9, BLOCK, C), BF16),
             pltpu.VMEM((C, TAPS), BF16),
-            packed,
-            packed,
-            packed,
+            pltpu.VMEM((3, HALF, LANES), F32),
+            pltpu.VMEM((3, HALF, LANES), F32),
+            pltpu.VMEM((BLOCK, LANES), F32),
+            pltpu.VMEM((BLOCK, LANES), F32),
             pltpu.VMEM((9, BLOCK, LANES), F32),
             pltpu.VMEM((2, HALF, LANES), F32),
             pltpu.VMEM((2, 2, Z - 1, HALF, LANES), BF16),
-            pltpu.VMEM((2, HALF, LANES), F32),
+            pltpu.VMEM((2, 2, HALF, LANES), F32),
             pltpu.VMEM((2, Z - 1, HALF, LANES), BF16),
             pltpu.VMEM((2, HALF, LANES), F32),
             pltpu.VMEM((2, HALF, LANES), BF16),
             pltpu.VMEM((2, HALF, LANES), BF16),
-            pltpu.SemaphoreType.DMA((C // PIECE,)),
+            pltpu.SemaphoreType.DMA,
             pltpu.SemaphoreType.DMA((10,)),
+            pltpu.SemaphoreType.DMA((5,)),
+            pltpu.SemaphoreType.DMA((5,)),
+            pltpu.SemaphoreType.DMA((3, 2)),
+            pltpu.SemaphoreType.DMA((3, 2)),
+            pltpu.SemaphoreType.REGULAR,
             pltpu.SemaphoreType.DMA((2, 2, Z - 1)),
-            pltpu.SemaphoreType.DMA((2,)),
+            pltpu.SemaphoreType.DMA((2, 2)),
             pltpu.SemaphoreType.DMA((2, Z - 1)),
             pltpu.SemaphoreType.DMA((2,)),
             pltpu.SemaphoreType.DMA((2,)),
@@ -486,7 +616,7 @@
         stale_step,
         jnp.transpose(latent, (0, 2, 1)),
         jnp.transpose(stale_rows[:, 0], (0, 1, 3, 4, 2)),
-        conv_weight.reshape(TAPS, C),
+        conv_weight[0],
         conv_bias,
         norm_gain,
         norm_shift,

time: 87.2 us -> 84 us (0.963)
  Pallas kernels: 84.9 us -> 82.2 us
    pallas_call x1, Pallas kernels: 84.9 us -> 82.2 us  [on_device(): pl.pallas_call(kernel, out_shape=pltpu.VMEM((2, CELLS, BLOCK), BF16), in_...]
where the time goes in v3:
time: 84 us; the launch traced here: 83.5 us
  Pallas kernels  82.2 us (98%)
    pallas_call x1, Pallas kernels, on_device(): pl.pallas_call(kernel, out_shape=pltpu.VMEM((2, CELLS, BLOCK), BF16), in_...  82.2 us

profile of v3, /device:TPU:25, one launch (start us, length us, event | category | flops | bytes accessed | tf_op | source)
XLA Modules:
  0.0 83.5 jit_solution(14576123772100527018)
XLA Ops:
  0.7 82.2 %segments.1 = bf16[2,64,80]{2,1,0:T(8,128)(2,1)S(1)} custom-call(s32[2]{0:T(128)} %order_hbm.1, s32[1]{0:T(128)S(6)} %copy.13.time_hbm, s32[1,2]{1,0:T(1,128)} %step_hbm.1, bf16[2,64,80]{2,1,0:T(8,128)(2,1)} %bitcast.15, bf16[4,2,2,32,80]{4,3,2,1,0:T(8,128)(2,1)} %bitcast.13, bf16[9,80,1280]{2,1,0:T(8,128)(2,1)} %bitcast.12, f32[1,80]{1,0:T(1,128)} %bias_hbm.1, ...), custom_call_target="tpu_custom_call" | custom-call | tf_op jit(solution)/shard_map/segments/pallas_call | solution.py:565
  82.9 0.6 copy.12

commit v4 on v3

--- a/solution.py
+++ b/solution.py
@@ -390,8 +390,12 @@
             block_copy(q, i).start()
 
     def finish(q):
-        for i in range(FAR):
-            block_copy(q, i).wait_send()
+
+        @pl.when(role < 4)
+        def _():
+            for i in range(FAR):
+                block_copy(q, i).wait_send()
+
         start(q, NEAR_CHUNK)
 
     @pl.when(is_first)
@@ -480,19 +484,17 @@
             for chunk in FAR_CHUNKS:
                 multiply(q, taps, chunk)
                 start(q, chunk)
-            multiply(q, taps, MIDDLE_CHUNKS[0])
+            own = multiply(q, taps, MIDDLE_CHUNKS[0] + MIDDLE_CHUNKS[1] + NEAR_CHUNK + (OWN,))[-1]
             start(q, MIDDLE_CHUNKS[0])
-            base_out_ref[q] = x + multiply(q, taps, (OWN,))[0] + packed_ref[2]
+            base_out_ref[q] = x + own + packed_ref[2]
 
             @pl.when(jnp.logical_not(stays))
             def _():
                 base_copy(q).start()
 
-            multiply(q, taps, MIDDLE_CHUNKS[1])
             start(q, MIDDLE_CHUNKS[1])
             back_out_ref[q] = x.astype(BF16)
             back_copy(q).start()
-            multiply(q, taps, NEAR_CHUNK)
             if q == 0:
                 next_halo(hidden)
             else:
@@ -534,6 +536,13 @@
     for q in range(2):
         for i in range(FAR, Z - 1):
             block_copy(q, i).wait_send()
+        if q == 1:
+
+            @pl.when(role >= 4)
+            def _():
+                for i in range(FAR):
+                    block_copy(1, i).wait_send()
+
         if q == 0:
 
             @pl.when(s > 0)

time: 84 us -> 83.8 us (level)
  no operation moved by 1% of the time
where the time goes in v4:
time: 83.8 us; the launch traced here: 83.5 us
  Pallas kernels  82.2 us (98%)
    pallas_call x1, Pallas kernels, on_device(): pl.pallas_call(kernel, out_shape=pltpu.VMEM((2, CELLS, BLOCK), BF16), in_...  82.2 us

profile of v4, /device:TPU:25, one launch (start us, length us, event | category | flops | bytes accessed | tf_op | source)
XLA Modules:
  0.0 83.5 jit_solution(11951058724650699887)
XLA Ops:
  0.7 82.2 %segments.1 = bf16[2,64,80]{2,1,0:T(8,128)(2,1)S(1)} custom-call(s32[2]{0:T(128)} %order_hbm.1, s32[1]{0:T(128)S(6)} %copy.13.time_hbm, s32[1,2]{1,0:T(1,128)} %step_hbm.1, bf16[2,64,80]{2,1,0:T(8,128)(2,1)} %bitcast.15, bf16[4,2,2,32,80]{4,3,2,1,0:T(8,128)(2,1)} %bitcast.13, bf16[9,80,1280]{2,1,0:T(8,128)(2,1)} %bitcast.12, f32[1,80]{1,0:T(1,128)} %bias_hbm.1, ...), custom_call_target="tpu_custom_call" | custom-call | tf_op jit(solution)/shard_map/segments/pallas_call | solution.py:574
  82.9 0.6 copy.12

commit v5 on v4

--- a/solution.py
+++ b/solution.py
@@ -391,7 +391,7 @@
 
     def finish(q):
 
-        @pl.when(role < 4)
+        @pl.when(role < 3)
         def _():
             for i in range(FAR):
                 block_copy(q, i).wait_send()
@@ -538,7 +538,7 @@
             block_copy(q, i).wait_send()
         if q == 1:
 
-            @pl.when(role >= 4)
+            @pl.when(role >= 3)
             def _():
                 for i in range(FAR):
                     block_copy(1, i).wait_send()

time: 83.8 us -> 83.8 us (level)
  no operation moved by 1% of the time
where the time goes in v5:
time: 83.8 us; the launch traced here: 83.5 us
  Pallas kernels  82.2 us (98%)
    pallas_call x1, Pallas kernels, on_device(): pl.pallas_call(kernel, out_shape=pltpu.VMEM((2, CELLS, BLOCK), BF16), in_...  82.2 us

profile of v5, /device:TPU:25, one launch (start us, length us, event | category | flops | bytes accessed | tf_op | source)
XLA Modules:
  0.0 83.5 jit_solution(3763065413760181946)
XLA Ops:
  0.7 82.2 %segments.1 = bf16[2,64,80]{2,1,0:T(8,128)(2,1)S(1)} custom-call(s32[2]{0:T(128)} %order_hbm.1, s32[1]{0:T(128)S(6)} %copy.13.time_hbm, s32[1,2]{1,0:T(1,128)} %step_hbm.1, bf16[2,64,80]{2,1,0:T(8,128)(2,1)} %bitcast.15, bf16[4,2,2,32,80]{4,3,2,1,0:T(8,128)(2,1)} %bitcast.13, bf16[9,80,1280]{2,1,0:T(8,128)(2,1)} %bitcast.12, f32[1,80]{1,0:T(1,128)} %bias_hbm.1, ...), custom_call_target="tpu_custom_call" | custom-call | tf_op jit(solution)/shard_map/segments/pallas_call | solution.py:574
  82.9 0.6 copy.12
